TPU v7x, 32 devices: a whole 2x2x4 slice. The times are simulated.
32 devices in a mesh: groups: 2 (over y), dp: 4 (over z), tensor: 4 (over x, core).
Axes of the slice: x: 2, y: 2, z: 4, core: 2. Of those that a mesh axis runs over, the one named last changes fastest.
Arguments:
- gate_preactivation: bfloat16 [1024, 14336], P(('groups', 'dp'), 'tensor'), parts along dimension 0, may hold values from -6 to 6
- up_preactivation: bfloat16 [1024, 14336], P(('groups', 'dp'), 'tensor'), parts along dimension 0, may hold values from -6 to 6
- quantized_weight_levels: int32 [14336, 4096], P('tensor', 'dp'), may hold values from 0 to 15
- absmax: float32 [14336, 64], P('tensor', 'dp'), may hold values from 0.004 to 0.04
- adapter_down_factor: bfloat16 [4, 14336, 64], P('dp', 'tensor'), may hold values from -0.046875 to 0.046875
- adapter_up_factor: bfloat16 [4, 64, 4096], P('dp', None, 'tensor'), may hold values from -0.75 to 0.75
- tenant_adapter_rank: int32 [4], replicated, may hold values from 16 to 64, as said below
- block_owner_tenant: int32 [8], P(('groups', 'dp')), parts along dimension 0, may hold values from 0 to 3
- block_live_rows: int32 [8], P(('groups', 'dp')), parts along dimension 0, may hold values from 32 to 128, as said below
- output_gradient: bfloat16 [1024, 4096], P(('groups', 'dp'), 'tensor'), parts along dimension 0, may hold values from -6 to 6
Outputs:
- projection_output: bfloat16 [1024, 4096], P(('groups', 'dp'), 'tensor'), parts along dimension 0
- gate_gradient: bfloat16 [1024, 14336], P(('groups', 'dp'), 'tensor'), parts along dimension 0
- up_gradient: bfloat16 [1024, 14336], P(('groups', 'dp'), 'tensor'), parts along dimension 0
- down_factor_gradient: float32 [8, 14336, 64], P(('groups', 'dp'), 'tensor'), parts along dimension 0
- up_factor_gradient: float32 [8, 64, 4096], P(('groups', 'dp'), None, 'tensor'), parts along dimension 0
There are 2 independent parts, one for each index of `groups`. A program takes and returns all parts, laid end to end along the dimension named above; an argument that names none is the same for every part. Nothing has to cross between parts.
Inputs may be any that keep to these rules, and one draw needn't show every extreme that they name: A tenant's adapter uses its first tenant_adapter_rank entries of the 64 rank slots; the values 64 // 4 and 64 both occur. `block_live_rows`: the live rows are the first ones of their block; some block is full and some holds the least.
All inputs are finite; a program needn't handle non-finite values.
Results may differ from a plain program's by a relative error of at most 0.015.
Values may be sent and summed in bfloat16 or wider, within the bound.
A program may use at most 128 MiB of HBM per device.

v0:
```python
import jax
import jax.numpy as jnp
from jax import lax
from jax.sharding import PartitionSpec as P

nf4_levels = (
    -1.0,
    -0.6961928009986877,
    -0.5250730514526367,
    -0.39491748809814453,
    -0.28444138169288635,
    -0.18477343022823334,
    -0.09105003625154495,
    0.0,
    0.07958029955625534,
    0.16093020141124725,
    0.24611230194568634,
    0.33791524171829224,
    0.44070982933044434,
    0.5626170039176941,
    0.7229568362236023,
    1.0,
)


def dequantize(quantized_weight_levels, absmax):
    values = jnp.zeros(quantized_weight_levels.shape, jnp.float32)
    for level_index, level_value in enumerate(nf4_levels):
        values = jnp.where(quantized_weight_levels == level_index, jnp.float32(level_value), values)
    rows_count, cols_count = quantized_weight_levels.shape
    scaled = (
        values.reshape(rows_count, absmax.shape[1], cols_count // absmax.shape[1])
        * absmax[:, :, None]
    )
    return scaled.reshape(rows_count, cols_count).astype(jnp.bfloat16)


def shards(
    gate_preactivation,
    up_preactivation,
    quantized_weight_levels,
    absmax,
    adapter_down_factor,
    adapter_up_factor,
    tenant_adapter_rank,
    block_owner_tenant,
    block_live_rows,
    output_gradient,
):
    token_rows, hidden_cols = gate_preactivation.shape
    width_portion = output_gradient.shape[1]
    block_count = block_owner_tenant.shape[0]
    block_size = token_rows // block_count
    tenants = tenant_adapter_rank.shape[0]
    adapter_rank_capacity = adapter_down_factor.shape[2]
    local_weight = dequantize(quantized_weight_levels, absmax)
    full_weight = lax.all_gather(local_weight, "dp", axis=1, tiled=True)
    adapters_a, adapters_b = (
        lax.all_gather(adapter_down_factor, "dp", axis=0, tiled=True),
        lax.all_gather(adapter_up_factor, "dp", axis=0, tiled=True),
    )
    tenant_hot = block_owner_tenant[:, None] == jnp.arange(tenants, dtype=jnp.int32)[None, :]
    block_rank = jnp.sum(jnp.where(tenant_hot, tenant_adapter_rank[None, :], 0), axis=1)
    block_absolute_scale = adapter_rank_capacity / (4.0 * block_rank.astype(jnp.float32))
    rank_keep = (jnp.arange(adapter_rank_capacity)[None, :] < block_rank[:, None]).astype(
        jnp.float32
    )
    live_rows = (jnp.arange(block_size)[None, :] < block_live_rows[:, None]).astype(jnp.float32)
    gate_vals = gate_preactivation.astype(jnp.float32).reshape(block_count, block_size, hidden_cols)
    up_vals = up_preactivation.astype(jnp.float32).reshape(block_count, block_size, hidden_cols)
    sigmoid_gate = jax.nn.sigmoid(gate_vals)
    silu_gate = gate_vals * sigmoid_gate
    hidden = (live_rows[:, :, None] * silu_gate * up_vals).astype(jnp.bfloat16)
    down_factor_rows = adapters_a[block_owner_tenant]
    up_factor_rows = adapters_b[block_owner_tenant]
    reduced_piece = jnp.einsum(
        "bkf,bfr->bkr", hidden, down_factor_rows, preferred_element_type=jnp.float32
    )
    reduced_rank_value = (
        lax.psum(reduced_piece.astype(jnp.bfloat16), "tensor").astype(jnp.float32)
        * rank_keep[:, None, :]
    ).astype(jnp.bfloat16)
    flat_hidden = hidden.reshape(token_rows, hidden_cols)
    partial_value = jnp.dot(flat_hidden, full_weight, preferred_element_type=jnp.float32)
    frozen_output = lax.psum_scatter(
        partial_value.astype(jnp.bfloat16), "tensor", scatter_dimension=1, tiled=True
    ).astype(jnp.float32)
    adapter_output = (
        jnp.einsum(
            "jof,jfs->jos", reduced_rank_value, up_factor_rows, preferred_element_type=jnp.float32
        )
        * block_absolute_scale[:, None, None]
    )
    projection_output = (frozen_output + adapter_output.reshape(token_rows, width_portion)).astype(
        jnp.bfloat16
    )
    full_grad = lax.all_gather(output_gradient, "tensor", axis=1, tiled=True)
    gradient_block_list = output_gradient.reshape(block_count, block_size, width_portion)
    backward_piece = jnp.einsum(
        "jpt,jyt->jpy", gradient_block_list, up_factor_rows, preferred_element_type=jnp.float32
    )
    backward_total = lax.psum(backward_piece.astype(jnp.bfloat16), "tensor").astype(jnp.float32)
    back_rank = (backward_total * (block_absolute_scale[:, None] * rank_keep)[:, None, :]).astype(
        jnp.bfloat16
    )
    grad_hidden = lax.dot_general(
        full_grad, full_weight, (((1,), (1,)), ((), ())), preferred_element_type=jnp.float32
    )
    grad_hidden = grad_hidden.reshape(block_count, block_size, hidden_cols)
    grad_hidden = grad_hidden + jnp.einsum(
        "bkr,bfr->bkf", back_rank, down_factor_rows, preferred_element_type=jnp.float32
    )
    grad_hidden = grad_hidden * live_rows[:, :, None]
    gate_gradient = (
        (grad_hidden * up_vals * sigmoid_gate * (1.0 + gate_vals * (1.0 - sigmoid_gate)))
        .astype(jnp.bfloat16)
        .reshape(token_rows, hidden_cols)
    )
    up_gradient = (grad_hidden * silu_gate).astype(jnp.bfloat16).reshape(token_rows, hidden_cols)
    hot_float = tenant_hot.astype(jnp.float32)
    term_a = jnp.einsum("bkf,bkr->bfr", hidden, back_rank, preferred_element_type=jnp.float32)
    second_summand = (
        jnp.einsum(
            "pqv,pqh->pvh",
            reduced_rank_value,
            gradient_block_list,
            preferred_element_type=jnp.float32,
        )
        * block_absolute_scale[:, None, None]
    )
    dense_a = jnp.einsum("be,bfr->efr", hot_float, term_a, precision=lax.Precision.HIGHEST)
    dense_b = jnp.einsum("be,brd->erd", hot_float, second_summand, precision=lax.Precision.HIGHEST)
    down_factor_gradient, up_factor_gradient = (
        lax.psum_scatter(
            dense_a.astype(jnp.bfloat16), "dp", scatter_dimension=0, tiled=True
        ).astype(jnp.float32),
        lax.psum_scatter(
            dense_b.astype(jnp.bfloat16), "dp", scatter_dimension=0, tiled=True
        ).astype(jnp.float32),
    )
    return (projection_output, gate_gradient, up_gradient, down_factor_gradient, up_factor_gradient)


def solution(mesh):
    placed = (
        P(("groups", "dp"), "tensor"),
        P(("groups", "dp"), "tensor"),
        P("tensor", "dp"),
        P("tensor", "dp"),
        P("dp", "tensor", None),
        P("dp", None, "tensor"),
        P(),
        P(("groups", "dp")),
        P(("groups", "dp")),
        P(("groups", "dp"), "tensor"),
    )
    return jax.shard_map(
        shards,
        mesh=mesh,
        in_specs=placed,
        out_specs=(
            P(("groups", "dp"), "tensor"),
            P(("groups", "dp"), "tensor"),
            P(("groups", "dp"), "tensor"),
            P(("groups", "dp"), "tensor", None),
            P(("groups", "dp"), None, "tensor"),
        ),
        check_vma=False,
    )
```

profile of v0, /device:TPU:0, one launch (start us, length us, event | category | flops | bytes accessed | tf_op | source)
XLA Modules:
  0.0 684.4 jit_solution(15112630354503725545)
XLA Ops:
  8.0 1.6 copy.43
  10.2 1.6 copy.42
  12.4 1.3 fusion.29
  15.5 1.2 compare_select_fusion
  17.3 24.5 %all_gather.14 = bf16[4,64,1024]{2,1,0:T(8,128)(2,1)S(1)} all-gather(bf16[1,64,1024]{2,1,0:T(8,128)(2,1)} %param.15), channel_id=1, replica_groups=mesh['groups'=2,'dp'=4,'tensor'=4] {'dp'}, dimensions={0}, use_global_device_ids=true | all-gather | bytes 655360 | tf_op jit(solution)/shard_map/all_gather | solution.py:60
  41.8 1.8 fusion.13
  44.2 18.2 %all-gather.6.cloned.1.call-done = bf16[4,3584,64]{1,2,0:T(8,128)(2,1)} async-done(((bf16[1,3584,64]{1,2,0:T(8,128)(2,1)}), bf16[4,3584,64]{1,2,0:T(8,128)(2,1)}) %all-gather.6.cloned.1.call-update) | async-done | bytes 1835024 | tf_op jit(solution)/shard_map/all_gather | solution.py:59
  62.4 1.3 fusion.12
  63.7 12.5 %all-reduce = (bf16[1,128,64]{1,2,0:T(8,128)(2,1)}, bf16[1,128,64]{1,2,0:T(8,128)(2,1)}) all-reduce(bf16[1,128,64]{1,2,0:T(8,128)(2,1)S(1)} %fusion.12, bf16[1,128,64]{1,2,0:T(8,128)(2,1)} %fusion.13), channel_id=1, replica_groups=mesh['groups'=2,'dp'=4,'tensor'=4] {'tensor'}, use_global_device_ids=true, to_apply=%region_1.2 | all-reduce | flops 16384 | bytes 65536 | tf_op jit(solution)/shard_map/psum | solution.py:80
  77.2 1.5 multiply_convert_fusion.2
  80.0 2.1 multiply_convert_fusion
  82.2 14.4 %copy.44 = s32[3584,1024]{0,1:T(8,128)} copy(s32[3584,1024]{1,0:T(8,128)} %param.12) | data formatting | bytes 29360128 | tf_op args[2]
  96.6 18.9 %fusion = bf16[3584,1024]{0,1:T(8,128)(2,1)} fusion(s32[3584,1024]{0,1:T(8,128)} %copy.44, f32[3584,16]{0,1:T(8,128)S(1)} %copy-done.1), kind=kLoop, calls=%fused_computation.1 | loop fusion | flops 124780544 | bytes 22249472 | tf_op jit(solution)/shard_map/convert_element_type | solution.py:35
  116.4 1.6 convert_element_type.116
  118.0 20.2 %reduce-scatter.6.cloned.1.call-done = bf16[1,3584,64]{1,2,0:T(8,128)(2,1)} async-done(((bf16[4,3584,64]{1,2,0:T(8,128)(2,1)}), bf16[1,3584,64]{1,2,0:T(8,128)(2,1)}) %reduce-scatter.6.cloned.1.call-update) | async-done | bytes 458768 | tf_op jit(solution)/shard_map/reduce_scatter | solution.py:134
  138.2 2.0 convert_element_type.114
  140.2 491.7 %all-gather.4.cloned.1.call-done = bf16[3584,4096]{0,1:T(8,128)(2,1)} async-done(((bf16[3584,1024]{0,1:T(8,128)(2,1)}), bf16[3584,4096]{0,1:T(8,128)(2,1)}) %all-gather.4.cloned.1.call-update) | async-done | bytes 29360144 | tf_op jit(solution)/shard_map/all_gather | solution.py:57
  631.9 16.2 %convolution_convert_fusion = bf16[128,4096]{1,0:T(8,128)(2,1)} fusion(bf16[128,3584]{0,1:T(8,128)(2,1)S(1)} %fusion.2, bf16[3584,4096]{0,1:T(8,128)(2,1)} %all-gather.4.cloned.1.call-done), kind=kOutput, calls=%fused_computation.5 | convolution fusion | flops 3758620672 | bytes 31326208 | tf_op jit(solution)/shard_map/dot_general | solution.py:84
  648.3 14.1 %convolution_bitcast_fusion = f32[128,3584]{0,1:T(8,128)S(1)} fusion(bf16[3584,4096]{0,1:T(8,128)(2,1)} %all-gather.4.cloned.1.call-done, bf16[128,4096]{1,0:T(8,128)(2,1)} %all-gather.8.cloned.1.call-done), kind=kOutput, calls=%fused_computation.4 | convolution fusion | flops 3758096384 | bytes 32243712 | tf_op jit(solution)/shard_map/dot_general | solution.py:106
  662.5 3.3 multiply_convert_fusion.1
  665.8 2.2 copy.61
  668.0 1.3 copy.62
  669.3 6.3 reduce-scatter.4.cloned.1.call-done
  675.6 2.0 fusion.11
  (36 shorter events, 6.3 us)
Async XLA Ops:
  7.2 69.1 %copy-start = (bf16[128,1024]{1,0:T(8,128)(2,1)S(1)}, bf16[128,1024]{1,0:T(8,128)(2,1)}, u32[]{:S(2)}) copy-start(bf16[128,1024]{1,0:T(8,128)(2,1)} %param.19) | copy-start | bytes 786436
  7.2 55.2 %all-gather.6.cloned.1.call-start = ((), (), s32[]{:S(2)}) async-start(), calls=%async_computation.5 | async-start | bytes 2293760 | tf_op jit(solution)/shard_map/all_gather | solution.py:59
  7.9 108.4 %reduce-scatter.8.cloned.1.call-start = ((), (), s32[]{:S(2)}) async-start(), calls=%async_computation.8 | async-start | bytes 655360 | tf_op jit(solution)/shard_map/reduce_scatter | solution.py:137
  15.5 28.0 %copy-start.5 = (f32[128]{0:T(128)}, f32[128]{0:T(128)S(1)}, u32[]{:S(2)}) copy-start(f32[128]{0:T(128)S(1)} %compare_convert_fusion) | copy-start | bytes 1540
  78.8 59.4 %reduce-scatter.6.cloned.1.call-start = ((), (), s32[]{:S(2)}) async-start(), calls=%async_computation.7 | async-start | bytes 2293760 | tf_op jit(solution)/shard_map/reduce_scatter | solution.py:134
  82.1 14.5 %copy-start.1 = (f32[3584,16]{0,1:T(8,128)S(1)}, f32[3584,16]{0,1:T(8,128)}, u32[]{:S(2)}) copy-start(f32[3584,16]{0,1:T(8,128)} %param.13) | copy-start | bytes 688132
  82.2 549.8 %all-gather.4.cloned.1.call-start = ((), (), s32[]{:S(2)}) async-start(), calls=%async_computation.3 | async-start | bytes 36700160 | tf_op jit(solution)/shard_map/all_gather | solution.py:57
  115.5 532.8 %all-gather.8.cloned.1.call-start = ((), (), s32[]{:S(2)}) async-start(), calls=%async_computation.6 | async-start | bytes 1310720 | tf_op jit(solution)/shard_map/all_gather | solution.py:97
  116.1 559.5 %reduce-scatter.4.cloned.1.call-start = ((), (), s32[]{:S(2)}) async-start(), calls=%async_computation.4 | async-start | bytes 1310720 | tf_op jit(solution)/shard_map/reduce_scatter | solution.py:85
  648.1 14.3 %copy-start.3 = (bf16[1,128,64]{1,2,0:T(8,128)(2,1)S(1)}, bf16[1,128,64]{1,2,0:T(8,128)(2,1)}, u32[]{:S(2)}) copy-start(bf16[1,128,64]{1,2,0:T(8,128)(2,1)} %get-tuple-element.43) | copy-start | bytes 49156
  648.2 14.3 %copy-start.6 = (f32[128]{0:T(128)S(1)}, f32[128]{0:T(128)}, u32[]{:S(2)}) copy-start(f32[128]{0:T(128)} %copy-done.5) | copy-start | bytes 1540
  648.2 14.3 %copy-start.7 = (f32[64]{0:T(128)S(1)}, f32[64]{0:T(128)}, u32[]{:S(2)}) copy-start(f32[64]{0:T(128)} %compare_select_fusion) | copy-start | bytes 772
  662.4 13.2 %copy-start.2 = (bf16[1,128,64]{1,2,0:T(8,128)(2,1)S(1)}, bf16[1,128,64]{1,2,0:T(8,128)(2,1)}, u32[]{:S(2)}) copy-start(bf16[1,128,64]{1,2,0:T(8,128)(2,1)} %get-tuple-element.42) | copy-start | bytes 49156
  662.5 13.1 %copy-start.4 = (f32[64]{0:T(128)S(1)}, f32[64]{0:T(128)}, u32[]{:S(2)}) copy-start(f32[64]{0:T(128)} %compare_convert_fusion.1) | copy-start | bytes 772
Sparse Core Ops, SparseCore 0:
  9.6 52.7 all-gather.5
  78.9 19.2 reduce-scatter.7
  100.5 37.6 reduce-scatter.5
  139.6 492.2 all-gather.3
  633.3 14.9 all-gather.7
  650.7 24.8 reduce-scatter.3
where the time goes:
time: 685 us; the launch traced here: 684 us
  waiting for transfers between devices  538 us (79%)
  matrix products  40.8 us (6%)
  blocking collectives  37.1 us (5%)
  other arithmetic  30.9 us (5%)
  local copies, waits for them, and re-layouts  21 us (3%)
  between operations  16.2 us (2%)
    all_gather x1, waiting for transfers between devices, shards(): full_weight = lax.all_gather(local_weight, 'dp', axis=1, tiled=True)  492 us
    all_gather x1, blocking collectives, shards(): lax.all_gather(adapter_up_factor, 'dp', axis=0, tiled=True)  24.5 us
    unnamed x21, local copies, waits for them, and re-layouts  21 us
    reduce_scatter x1, waiting for transfers between devices, shards(): lax.psum_scatter(dense_a.astype(jnp.bfloat16), 'dp', scatter_dimension=0,...  20.2 us
    convert_element_type x1, other arithmetic, dequantize(): return scaled.reshape(rows_count, cols_count).astype(jnp.bfloat16)  18.9 us
    all_gather x1, waiting for transfers between devices, shards(): lax.all_gather(adapter_down_factor, 'dp', axis=0, tiled=True)  18.2 us
    dot_general x1, matrix products, shards(): jnp.dot(flat_hidden, full_weight, preferred_element_type=jnp.float32)  16.2 us
    dot_general x1, matrix products, shards(): lax.dot_general(full_grad, full_weight, (((1,), (1,)), ((), ())), preferr...  14.1 us
  transfers between devices with their start and end apart: 6, of which 5 were waited for; matrix products, arithmetic and copies ran while one was open for 13% of the time, Pallas kernels for 0%

commit v1 on v0

v1 whole, which is shorter than its diff:
```python
import jax
import jax.numpy as jnp
from jax import lax
from jax.sharding import PartitionSpec as P

nf4_levels = (
    -1.0,
    -0.6961928009986877,
    -0.5250730514526367,
    -0.39491748809814453,
    -0.28444138169288635,
    -0.18477343022823334,
    -0.09105003625154495,
    0.0,
    0.07958029955625534,
    0.16093020141124725,
    0.24611230194568634,
    0.33791524171829224,
    0.44070982933044434,
    0.5626170039176941,
    0.7229568362236023,
    1.0,
)


def dequantize(quantized_weight_levels, absmax):
    values = jnp.zeros(quantized_weight_levels.shape, jnp.float32)
    for level_index, level_value in enumerate(nf4_levels):
        values = jnp.where(quantized_weight_levels == level_index, jnp.float32(level_value), values)
    rows_count, cols_count = quantized_weight_levels.shape
    scaled = (
        values.reshape(rows_count, absmax.shape[1], cols_count // absmax.shape[1])
        * absmax[:, :, None]
    )
    return scaled.reshape(rows_count, cols_count).astype(jnp.bfloat16)


def shards(
    gate_preactivation,
    up_preactivation,
    quantized_weight_levels,
    absmax,
    adapter_down_factor,
    adapter_up_factor,
    tenant_adapter_rank,
    block_owner_tenant,
    block_live_rows,
    output_gradient,
):
    f32, bf16 = jnp.float32, jnp.bfloat16
    n_dp, n_tensor = lax.axis_size("dp"), lax.axis_size("tensor")
    dp, tensor = lax.axis_index("dp"), lax.axis_index("tensor")
    rows, hidden_cols = gate_preactivation.shape
    width = output_gradient.shape[1]
    blocks = block_owner_tenant.shape[0]
    block_size = rows // blocks
    slots = adapter_down_factor.shape[2]
    swap = [(i * n_tensor + m, m * n_tensor + i) for i in range(n_dp) for m in range(n_tensor)]

    packed = jnp.concatenate([output_gradient, adapter_up_factor[0]], axis=0)
    packed = lax.ppermute(packed, ("dp", "tensor"), swap)
    packed = lax.all_gather(packed, "tensor", axis=0, tiled=False)
    all_grad = packed[:, :rows].reshape(n_tensor * rows, width)
    all_up_factor = packed[:, rows:]

    owner = lax.all_gather(block_owner_tenant, "dp", axis=0, tiled=True)
    row_tenant = jnp.repeat(owner, block_size)
    row_rank = tenant_adapter_rank[row_tenant]
    row_scale = slots / (4.0 * row_rank.astype(f32))
    row_keep = (jnp.arange(slots)[None, :] < row_rank[:, None]).astype(f32)
    mine = (row_tenant == dp).astype(f32)[:, None]
    first = tensor * rows

    def own_rows(value):
        return lax.dynamic_slice_in_dim(value, first, rows, 0)

    own_up_factor = jnp.repeat(all_up_factor[lax.dynamic_slice_in_dim(owner, tensor * blocks, blocks, 0)], 1, axis=0)
    own_grad = own_rows(all_grad).reshape(blocks, block_size, width)
    piece = jnp.einsum("jpt,jyt->jpy", own_grad, own_up_factor, preferred_element_type=f32)
    spread = lax.dynamic_update_slice_in_dim(
        jnp.zeros((n_tensor * rows, slots), bf16), piece.reshape(rows, slots).astype(bf16), first, 0
    )
    back_rank = lax.psum(spread, ("dp", "tensor")).astype(f32) * (row_scale[:, None] * row_keep)
    back_rank = back_rank.astype(bf16)
    mine_back = back_rank * mine.astype(bf16)

    gate_vals = gate_preactivation.astype(f32)
    up_vals = up_preactivation.astype(f32)
    live = (jnp.arange(block_size)[None, :] < block_live_rows[:, None]).astype(f32).reshape(rows, 1)
    sigmoid_gate = jax.nn.sigmoid(gate_vals)
    silu_gate = gate_vals * sigmoid_gate
    hidden = (live * silu_gate * up_vals).astype(bf16)
    all_hidden = lax.all_gather(hidden, "dp", axis=0, tiled=True)

    weight = dequantize(quantized_weight_levels, absmax)
    down_factor = adapter_down_factor[0]

    partial_grad = lax.dot_general(
        all_grad, weight, (((1,), (1,)), ((), ())), preferred_element_type=f32
    ) + lax.dot_general(mine_back, down_factor, (((1,), (1,)), ((), ())), preferred_element_type=f32)
    grad_hidden = lax.psum_scatter(
        partial_grad.astype(bf16), "dp", scatter_dimension=0, tiled=True
    ).astype(f32)

    low = jnp.dot(all_hidden, down_factor, preferred_element_type=f32) * (mine * row_keep)
    low_rank = lax.psum(low.astype(bf16), ("dp", "tensor"))
    partial_out = jnp.dot(all_hidden, weight, preferred_element_type=f32)
    frozen = lax.psum_scatter(
        partial_out.astype(bf16), "tensor", scatter_dimension=0, tiled=True
    ).astype(f32)
    adapter_out = jnp.einsum(
        "jof,jfs->jos",
        own_rows(low_rank).reshape(blocks, block_size, slots),
        own_up_factor,
        preferred_element_type=f32,
    ).reshape(rows, width) * own_rows(row_scale)[:, None]
    projection_output = lax.ppermute((frozen + adapter_out).astype(bf16), ("dp", "tensor"), swap)

    down_factor_gradient = lax.dot_general(
        all_hidden, mine_back, (((0,), (0,)), ((), ())), preferred_element_type=f32
    )[None]
    other = (row_tenant == tensor).astype(bf16)[:, None]
    up_term = lax.dot_general(
        low_rank * other, all_grad, (((0,), (0,)), ((), ())), preferred_element_type=f32
    ) * (slots / (4.0 * tenant_adapter_rank[tensor].astype(f32)))
    up_factor_gradient = lax.ppermute(up_term.astype(bf16), ("dp", "tensor"), swap).astype(f32)[None]

    grad_hidden = grad_hidden * live
    gate_gradient = (
        grad_hidden * up_vals * sigmoid_gate * (1.0 + gate_vals * (1.0 - sigmoid_gate))
    ).astype(bf16)
    up_gradient = (grad_hidden * silu_gate).astype(bf16)
    return (projection_output, gate_gradient, up_gradient, down_factor_gradient, up_factor_gradient)


def solution(mesh):
    placed = (
        P(("groups", "dp"), "tensor"),
        P(("groups", "dp"), "tensor"),
        P("tensor", "dp"),
        P("tensor", "dp"),
        P("dp", "tensor", None),
        P("dp", None, "tensor"),
        P(),
        P(("groups", "dp")),
        P(("groups", "dp")),
        P(("groups", "dp"), "tensor"),
    )
    return jax.shard_map(
        shards,
        mesh=mesh,
        in_specs=placed,
        out_specs=(
            P(("groups", "dp"), "tensor"),
            P(("groups", "dp"), "tensor"),
            P(("groups", "dp"), "tensor"),
            P(("groups", "dp"), "tensor", None),
            P(("groups", "dp"), None, "tensor"),
        ),
        check_vma=False,
    )
```

time: 685 us -> 335 us (0.49)
  waiting for transfers between devices: 538 us -> 201 us
  matrix products: 40.8 us -> 29.9 us
  blocking collectives: 37.1 us -> 29.8 us
    all_gather x3 -> x2, waiting for transfers between devices: 510 us -> 38.7 us  [the longest x1 38.7 us: shards(): all_hidden = lax.all_gather(hidden, 'dp', axis=0, tiled=True)]
    psum x0 -> x1, waiting for transfers between devices: none -> 76.6 us  [shards(): low_rank = lax.psum(low.astype(bf16), ('dp', 'tensor'))]
    reduce_scatter x3 -> x2, waiting for transfers between devices: 26.6 us -> 85.6 us  [the longest x1 70.4 us: shards(): lax.psum_scatter(partial_grad.astype(bf16), 'dp', scatter_dimension=0, ti...]
    unnamed x0 -> x1, blocking collectives: none -> 29.8 us
    all_gather x1 -> x0, blocking collectives: 24.5 us -> none  [shards(): lax.all_gather(adapter_up_factor, 'dp', axis=0, tiled=True)]
    psum x1 -> x0, blocking collectives: 12.5 us -> none  [shards(): lax.psum(reduced_piece.astype(jnp.bfloat16), 'tensor').astype(jnp.float32)]
    dot_general x8, matrix products: 40.8 us -> 29.9 us  [the longest x1 9.16 us: shards(): partial_out = jnp.dot(all_hidden, weight, preferred_element_type=f32)]
    unnamed x21 -> x23, local copies, waits for them, and re-layouts: 21 us -> 17.9 us
  transfers between devices with their start and end apart: 6 -> 8, of which waited for: 5 -> 4; matrix products, arithmetic and copies ran while one was open for 13% -> 22% of each run, Pallas kernels for 0% -> 0%
where the time goes in v1:
time: 335 us; the launch traced here: 333 us
  waiting for transfers between devices  201 us (60%)
  matrix products  29.9 us (9%)
  other arithmetic  29.8 us (9%)
  blocking collectives  29.8 us (9%)
  local copies, waits for them, and re-layouts  22.5 us (7%)
  between operations  18 us (5%)
    psum x1, waiting for transfers between devices, shards(): low_rank = lax.psum(low.astype(bf16), ('dp', 'tensor'))  76.6 us
    reduce_scatter x1, waiting for transfers between devices, shards(): lax.psum_scatter(partial_grad.astype(bf16), 'dp', scatter_dimension=0, ti...  70.4 us
    all_gather x1, waiting for transfers between devices, shards(): all_hidden = lax.all_gather(hidden, 'dp', axis=0, tiled=True)  38.7 us
    unnamed x1, blocking collectives  29.8 us
    convert_element_type x1, other arithmetic, dequantize(): return scaled.reshape(rows_count, cols_count).astype(jnp.bfloat16)  19 us
    unnamed x23, local copies, waits for them, and re-layouts  17.9 us
    reduce_scatter x1, waiting for transfers between devices, shards(): lax.psum_scatter(partial_out.astype(bf16), 'tensor', scatter_dimension=0,...  15.3 us
    dot_general x1, matrix products, shards(): partial_out = jnp.dot(all_hidden, weight, preferred_element_type=f32)  9.16 us
  transfers between devices with their start and end apart: 8, of which 4 were waited for; matrix products, arithmetic and copies ran while one was open for 22% of the time, Pallas kernels for 0%

profile of v1, /device:TPU:0, one launch (start us, length us, event | category | flops | bytes accessed | tf_op | source)
XLA Modules:
  0.0 333.3 jit_solution(12871028249977174081)
XLA Ops:
  7.2 1.1 pad_maximum_fusion
  9.0 0.7 copy-done.5
  10.5 3.1 fusion.1
  14.3 1.2 dynamic-slice.4
  15.6 0.8 dynamic-update-slice.1
  16.3 29.8 %all-reduce = s32[4]{0:T(128)S(1)} all-reduce(s32[4]{0:T(128)S(1)} %dynamic-update-slice.1), channel_id=1, replica_groups=mesh['groups'=2,'dp'=4,'tensor'=4] {'dp'}, use_global_device_ids=true, to_apply=%add | all-reduce | flops 4 | bytes 32
  46.1 14.4 %copy.16 = s32[3584,1024]{0,1:T(8,128)} copy(s32[3584,1024]{1,0:T(8,128)} %param.12) | data formatting | bytes 29360128 | tf_op args[2]
  62.5 19.0 %fusion = bf16[3584,1024]{0,1:T(8,128)(2,1)} fusion(s32[3584,1024]{0,1:T(8,128)} %copy.16, f32[3584,16]{0,1:T(8,128)S(1)} %copy-done.7), kind=kLoop, calls=%fused_computation.1 | loop fusion | flops 124780544 | bytes 22249472 | tf_op jit(solution)/shard_map/convert_element_type | solution.py:35
  82.9 2.5 compare_select_fusion.1
  85.4 1.1 slice.22
  86.5 1.5 slice.23
  88.3 38.7 %all-gather.4.cloned.1.call-done = bf16[512,3584]{1,0:T(8,128)(2,1)} async-done(((bf16[128,3584]{1,0:T(8,128)(2,1)}), bf16[512,3584]{1,0:T(8,128)(2,1)}) %all-gather.4.cloned.1.call-update) | async-done | bytes 3670032 | tf_op jit(solution)/shard_map/all_gather | solution.py:93
  127.0 3.9 %fusion.12 = bf16[512,64]{0,1:T(8,128)(2,1)} fusion(bf16[512,3584]{1,0:T(8,128)(2,1)} %all-gather.4.cloned.1.call-done, bf16[1,3584,64]{1,2,0:T(8,128)(2,1)S(1)} %copy-done, f32[512]{0:T(512)S(1)} %broadcast_bitcast_fusion, s32[512]{0:T(512)S(1)} %bitcast.50), kind=kOutput, calls=%fused_computation.26 | convolution fusion | flops 235012096 | bytes 4198400 | tf_op jit(solution)/shard_map/dot_general | solution.py:105
  130.9 9.2 %convolution_convert_fusion = bf16[512,1024]{1,0:T(8,128)(2,1)} fusion(bf16[512,3584]{1,0:T(8,128)(2,1)} %all-gather.4.cloned.1.call-done, bf16[3584,1024]{0,1:T(8,128)(2,1)} %fusion), kind=kOutput, calls=%fused_computation.19 | convolution fusion | flops 3758620672 | bytes 12058624 | tf_op jit(solution)/shard_map/dot_general | solution.py:107
  140.2 76.6 %all-reduce.4.cloned.1.call-done = (bf16[512,64]{0,1:T(8,128)(2,1)}, bf16[512,64]{0,1:T(8,128)(2,1)}) async-done(((bf16[512,64]{0,1:T(8,128)(2,1)}, bf16[512,64]{0,1:T(8,128)(2,1)}), (bf16[512,64]{0,1:T(8,128)(2,1)}, bf16[512,64]{0,1:T(8,128)(2,1)})) %all-reduce.4.cloned.1.call-update) | async-done | bytes 131088 | tf_op jit(solution)/shard_map/psum | solution.py:106
  216.8 2.0 fusion.14
  218.8 8.5 %add_convert_fusion = bf16[512,3584]{1,0:T(8,128)(2,1)} fusion(f32[512,3584]{1,0:T(8,128)S(1)} %fusion.14, bf16[512,1024]{1,0:T(8,128)(2,1)S(1)} %bitcast.46, bf16[3584,1024]{0,1:T(8,128)(2,1)} %fusion), kind=kOutput, calls=%fused_computation.2 | convolution fusion | flops 3761766400 | bytes 19398656 | tf_op jit(solution)/shard_map/dot_general | solution.py:98
  228.8 1.1 fusion.11
  230.6 15.3 %reduce-scatter.3.cloned.1.call-done = bf16[128,1024]{1,0:T(8,128)(2,1)} async-done(((bf16[512,1024]{1,0:T(8,128)(2,1)}), bf16[128,1024]{1,0:T(8,128)(2,1)}) %reduce-scatter.3.cloned.1.call-update) | async-done | bytes 262160 | tf_op jit(solution)/shard_map/reduce_scatter | solution.py:108
  245.9 1.3 fusion.10
  247.9 3.7 %convolution_bitcast_fusion = f32[1,3584,64]{1,2,0:T(8,128)} fusion(bf16[512,3584]{1,0:T(8,128)(2,1)} %all-gather.4.cloned.1.call-done, bf16[512,64]{0,1:T(8,128)(2,1)S(1)} %copy-done.4, f32[512]{0:T(512)S(1)} %multiply_divide_fusion, s32[512]{0:T(512)S(1)} %bitcast.53, bf16[512]{0:T(512)(128)(2,1)S(1)} %bitcast_convert_fusion.1), kind=kOutput, calls=%fused_computation.3 | convolution fusion | flops 235175936 | bytes 4658176 | tf_op jit(solution)/shard_map/dot_general | solution.py:119
  251.6 0.7 bitcast_convert_fusion
  252.3 70.4 %reduce-scatter.5.cloned.1.call-done = bf16[128,3584]{1,0:T(8,128)(2,1)} async-done(((bf16[512,3584]{1,0:T(8,128)(2,1)}), bf16[128,3584]{1,0:T(8,128)(2,1)}) %reduce-scatter.5.cloned.1.call-update) | async-done | bytes 917520 | tf_op jit(solution)/shard_map/reduce_scatter | solution.py:101
  322.7 3.4 %multiply_convert_fusion = (bf16[128,3584]{1,0:T(8,128)(2,1)}, bf16[128,3584]{1,0:T(8,128)(2,1)}) fusion(bf16[128,3584]{1,0:T(8,128)(2,1)} %reduce-scatter.5.cloned.1.call-done, f32[128]{0:T(128)S(1)} %compare_convert_fusion.2, bf16[128,3584]{1,0:T(8,128)(2,1)S(1)} %copy-done.2, bf16[128,3584]{1,0:T(8,128)(2,1)S(1)} %copy-done.1), kind=kLoop, calls=%fused_computation.17 | loop fusion | flops 7798784 | bytes 4588032 | tf_op jit(solution)/shard_map/convert_element_type | solution.py:132
  (48 shorter events, 5.4 us)
Async XLA Ops:
  7.2 119.8 %copy-start = (bf16[1,3584,64]{1,2,0:T(8,128)(2,1)S(1)}, bf16[1,3584,64]{1,2,0:T(8,128)(2,1)}, u32[]{:S(2)}) copy-start(bf16[1,3584,64]{1,2,0:T(8,128)(2,1)} %param.14) | copy-start | bytes 1376260
  7.2 78.2 %all-gather.6.cloned.1.call-start = ((), (), s32[]{:S(2)}) async-start(), calls=%async_computation.5 | async-start | bytes 1966080 | tf_op jit(solution)/shard_map/all_gather | solution.py:62
  8.3 0.7 collective-permute-start
  9.0 0.7 copy-start.5
  9.8 117.2 %all-gather.4.cloned.1.call-start = ((), (), s32[]{:S(2)}) async-start(), calls=%async_computation.2 | async-start | bytes 4587520 | tf_op jit(solution)/shard_map/all_gather | solution.py:93
  13.6 203.2 %all-reduce.4.cloned.1.call-start = ((), (), s32[]{:S(2)}) async-start(), calls=%async_computation.6 | async-start | bytes 262144 | tf_op jit(solution)/shard_map/psum | solution.py:106
  46.1 16.3 %copy-start.7 = (f32[3584,16]{0,1:T(8,128)S(1)}, f32[3584,16]{0,1:T(8,128)}, u32[]{:S(2)}) copy-start(f32[3584,16]{0,1:T(8,128)} %param.13) | copy-start | bytes 688132
  62.5 19.6 %copy-start.8 = (s32[4]{0:T(128)S(1)}, s32[4]{0:T(128)}, u32[]{:S(2)}) copy-start(s32[4]{0:T(128)} %param.16) | copy-start | bytes 52
  86.5 1.5 copy-start.3
  88.2 42.6 %copy-start.6 = (bf16[512,64]{0,1:T(8,128)(2,1)}, bf16[512,64]{0,1:T(8,128)(2,1)S(1)}, u32[]{:S(2)}) copy-start(bf16[512,64]{0,1:T(8,128)(2,1)S(1)} %fusion.13) | copy-start | bytes 196612
  130.9 115.0 %reduce-scatter.3.cloned.1.call-start = ((), (), s32[]{:S(2)}) async-start(), calls=%async_computation.3 | async-start | bytes 1310720 | tf_op jit(solution)/shard_map/reduce_scatter | solution.py:108
  140.1 182.5 %reduce-scatter.5.cloned.1.call-start = ((), (), s32[]{:S(2)}) async-start(), calls=%async_computation.4 | async-start | bytes 4587520 | tf_op jit(solution)/shard_map/reduce_scatter | solution.py:101
  218.8 29.0 %copy-start.4 = (bf16[512,64]{0,1:T(8,128)(2,1)S(1)}, bf16[512,64]{0,1:T(8,128)(2,1)}, u32[]{:S(2)}) copy-start(bf16[512,64]{0,1:T(8,128)(2,1)} %get-tuple-element.17) | copy-start | bytes 196612
  227.3 95.3 %copy-start.1 = (bf16[128,3584]{1,0:T(8,128)(2,1)S(1)}, bf16[128,3584]{1,0:T(8,128)(2,1)}, u32[]{:S(2)}) copy-start(bf16[128,3584]{1,0:T(8,128)(2,1)} %param.11) | copy-start | bytes 2752516
  227.3 95.3 %copy-start.2 = (bf16[128,3584]{1,0:T(8,128)(2,1)S(1)}, bf16[128,3584]{1,0:T(8,128)(2,1)}, u32[]{:S(2)}) copy-start(bf16[128,3584]{1,0:T(8,128)(2,1)} %param.10) | copy-start | bytes 2752516
  229.9 21.6 %collective-permute-start.2 = (bf16[64,1024]{1,0:T(8,128)(2,1)S(1)}, bf16[64,1024]{1,0:T(8,128)(2,1)S(1)}, u32[]{:S(2)}, u32[]{:S(2)}) collective-permute-start(bf16[64,1024]{1,0:T(8,128)(2,1)S(1)} %fusion.11), channel_id=1, source_target_pairs={{0,0},{1,4},{2,8},{3,12},{4,1},{5,5},{6,9},{7,13},{8,2},{9,6},{10,... | collective-permute-start | bytes 393224 | tf_op jit(solution)/shard_map/ppermute | solution.py:126
  247.2 5.1 %collective-permute-start.1 = (bf16[128,1024]{1,0:T(8,128)(2,1)S(1)}, bf16[128,1024]{1,0:T(8,128)(2,1)S(1)}, u32[]{:S(2)}, u32[]{:S(2)}) collective-permute-start(bf16[128,1024]{1,0:T(8,128)(2,1)S(1)} %fusion.10), channel_id=1, source_target_pairs={{0,0},{1,4},{2,8},{3,12},{4,1},{5,5},{6,9},{7,13},{8,2},{9,6},{10,... | collective-permute-start | bytes 786440 | tf_op jit(solution)/shard_map/ppermute | solution.py:117
Sparse Core Ops, SparseCore 0:
  10.1 42.4 all-gather.5
  54.8 72.1 all-gather.3
  131.1 85.7 all-reduce.3
  219.2 26.6 reduce-scatter.2
  248.1 74.4 reduce-scatter.4

commit v2 on v1

v2 whole, which is shorter than its diff:
```python
import functools

import jax
import jax.numpy as jnp
from jax import lax
from jax.experimental import pallas as pl
from jax.experimental.pallas import tpu as pltpu
from jax.sharding import PartitionSpec as P

MESH = pl.DeviceIdType.MESH
F32, BF16 = jnp.float32, jnp.bfloat16
CHUNKS = 7
LAG = 2

nf4_levels = (
    -1.0,
    -0.6961928009986877,
    -0.5250730514526367,
    -0.39491748809814453,
    -0.28444138169288635,
    -0.18477343022823334,
    -0.09105003625154495,
    0.0,
    0.07958029955625534,
    0.16093020141124725,
    0.24611230194568634,
    0.33791524171829224,
    0.44070982933044434,
    0.5626170039176941,
    0.7229568362236023,
    1.0,
)


def lookup(code):
    bits = [(code & (1 << b)) != 0 for b in range(4)]
    values = [jnp.float32(v) for v in nf4_levels]
    for bit in bits:
        values = [jnp.where(bit, values[i + 1], values[i]) for i in range(0, len(values), 2)]
    return values[0]


def dot_t(a, b):
    return lax.dot_general(a, b, (((1,), (1,)), ((), ())), preferred_element_type=F32)


def dot_0(a, b):
    return lax.dot_general(a, b, (((0,), (0,)), ((), ())), preferred_element_type=F32)


def dot(a, b):
    return jnp.dot(a, b, preferred_element_type=F32)


def kernel(
    nd,
    nt,
    rank_ref,
    owner_ref,
    live_ref,
    gate_ref,
    up_ref,
    levels_ref,
    absmax_ref,
    down_ref,
    up_factor_ref,
    grad_ref,
    out_ref,
    gate_grad_ref,
    up_grad_ref,
    down_grad_ref,
    up_grad_factor_ref,
    codes,
    weight,
    hid,
    all_grad,
    own_up,
    part,
    from_left,
    from_right,
    base,
    low,
    back_src,
    back_dst,
    back_own,
    back_mask_src,
    back_mask,
    low_src,
    low_dst,
    low_own,
    low_mask,
    base_src,
    base_dst,
    out_src,
    up_term,
    up_land,
    code_sem,
    local_sem,
    swap_send,
    swap_recv,
    hid_send,
    hid_recv,
    part_send,
    left_recv,
    right_recv,
    dp_send,
    dp_recv,
    tensor_send,
    tensor_recv,
):
    z, k = lax.axis_index("dp"), lax.axis_index("tensor")
    rows, hidden_cols = gate_ref.shape
    width = grad_ref.shape[1]
    slots = down_ref.shape[1]
    fc = hidden_cols // CHUNKS
    off_diagonal = z != k

    def remote(src, dst, send, recv, device):
        return pltpu.make_async_remote_copy(
            src_ref=src,
            dst_ref=dst,
            send_sem=send,
            recv_sem=recv,
            device_id=device,
            device_id_type=MESH,
        )

    def code_copy(c):
        slot = lax.rem(c, 2)
        return pltpu.make_async_copy(
            levels_ref.at[pl.ds(c * fc, fc)], codes.at[slot], code_sem.at[slot]
        )

    code_copy(0).start()
    code_copy(1).start()

    barrier = pltpu.get_barrier_semaphore()
    for o in range(1, nd):
        pl.semaphore_signal(
            barrier, inc=1, device_id={"dp": lax.rem(z + o, nd)}, device_id_type=MESH
        )
    for o in range(1, nt):
        pl.semaphore_signal(
            barrier, inc=1, device_id={"tensor": lax.rem(k + o, nt)}, device_id_type=MESH
        )

    @pl.when(off_diagonal)
    def _():
        pl.semaphore_signal(
            barrier, inc=1, device_id={"dp": k, "tensor": z}, device_id_type=MESH
        )
        pl.semaphore_wait(barrier, nd - 1 + nt - 1 + 1)

    @pl.when(jnp.logical_not(off_diagonal))
    def _():
        pl.semaphore_wait(barrier, nd - 1 + nt - 1)

    def swap_copy(which, src, dst):
        return remote(
            src, dst, swap_send.at[which], swap_recv.at[which], {"dp": k, "tensor": z}
        )

    def swap_start(which, src, dst):
        @pl.when(off_diagonal)
        def _():
            swap_copy(which, src, dst).start()

        @pl.when(jnp.logical_not(off_diagonal))
        def _():
            copy = pltpu.make_async_copy(src, dst, local_sem.at[which])
            copy.start()
            copy.wait()

    def swap_wait(which, src, dst):
        @pl.when(off_diagonal)
        def _():
            copy = swap_copy(which, src, dst)
            copy.wait()

    def spread(axis, which, source, target):
        n, me = (nd, z) if axis == "dp" else (nt, k)
        send, recv = (dp_send, dp_recv) if axis == "dp" else (tensor_send, tensor_recv)
        copies = []
        for o in range(1, n):
            peer = lax.rem(me + o, n)
            copies.append(
                remote(source(peer), target, send.at[which, o], recv.at[which, o], {axis: peer})
            )
        return copies

    def start(copies):
        for copy in copies:
            copy.start()

    def finish(copies):
        for copy in copies:
            copy.wait()

    swap_start(0, grad_ref, all_grad.at[z])
    swap_start(1, up_factor_ref, own_up)

    live = (
        lax.broadcasted_iota(jnp.int32, (rows, 1), 0) < live_ref[0]
    ).astype(F32)

    def hid_copy(direction, s, c):
        peer = z + 1 if direction == 0 else z - 1
        return remote(
            hid.at[s, c],
            hid.at[s, c],
            hid_send.at[direction, s, c],
            hid_recv.at[s, c],
            {"dp": peer},
        )

    def make_hidden(c, _):
        cols = pl.ds(pl.multiple_of(c * fc, fc), fc)
        gate = gate_ref[:, cols].astype(F32)
        up = up_ref[:, cols].astype(F32)
        hid[z, c] = (live * (gate * jax.nn.sigmoid(gate)) * up).astype(BF16)

        @pl.when(z + 1 < nd)
        def _():
            hid_copy(0, z, c).start()

        @pl.when(z > 0)
        def _():
            hid_copy(1, z, c).start()

        return 0

    lax.fori_loop(0, CHUNKS, make_hidden, 0)

    tile = 32
    blocks_per_scale = width // absmax_ref.shape[1]
    lanes = lax.broadcasted_iota(jnp.int32, (tile, 128), 1)

    def dequantize(c):
        code_copy(c).wait()
        slot = lax.rem(c, 2)

        def step(t, _):
            r = pl.ds(pl.multiple_of(t * tile, tile), tile)
            scale = absmax_ref[pl.ds(pl.multiple_of(c * fc + t * tile, tile), tile), :]
            for g in range(width // 128):
                cols = slice(g * 128, (g + 1) * 128)
                per = 128 // blocks_per_scale
                spreaded = scale[:, g * per : g * per + 1]
                for q in range(1, per):
                    spreaded = jnp.where(
                        lanes < q * blocks_per_scale,
                        spreaded,
                        scale[:, g * per + q : g * per + q + 1],
                    )
                weight[c, r, cols] = (lookup(codes[slot, r, cols]) * spreaded).astype(BF16)
            return 0

        lax.fori_loop(0, fc // tile, step, 0)

        @pl.when(c + 2 < CHUNKS)
        def _():
            code_copy(c + 2).start()

    def forward(s, c, first):
        value = hid[s, c]
        down = down_ref[pl.ds(pl.multiple_of(c * fc, fc), fc), :]
        if first:

            @pl.when(c == 0)
            def _():
                base[s] = jnp.zeros((rows, width), F32)
                low[s] = jnp.zeros((rows, slots), F32)

        base[s] += dot(value, weight[c])
        low[s] += dot(value, down)

    def gather_step(n, first):
        h = 1 + lax.div(n, CHUNKS)
        c = lax.rem(n, CHUNKS)

        @pl.when(z - h >= 0)
        def _():
            hid_copy(0, z - h, c).wait_recv()

            @pl.when(z + 1 < nd)
            def _():
                hid_copy(0, z - h, c).start()

        @pl.when(z + h < nd)
        def _():
            hid_copy(1, z + h, c).wait_recv()

            @pl.when(z > 0)
            def _():
                hid_copy(1, z + h, c).start()

        @pl.when(z - h >= 0)
        def _():
            forward(z - h, c, True)

        @pl.when(z + h < nd)
        def _():
            forward(z + h, c, True)

    def early(n, _):
        dequantize(n)
        forward(z, n, True)
        gather_step(n, True)
        return 0

    def partial(d, c):
        down = down_ref[pl.ds(pl.multiple_of(c * fc, fc), fc), :]
        return dot_t(all_grad[d], weight[c]) + dot_t(back_mask[d], down)

    def part_copy(direction, d, c):
        landing, recv = (from_left, left_recv) if direction == 0 else (from_right, right_recv)
        return remote(
            part.at[d, c],
            landing.at[d, c],
            part_send.at[d, c],
            recv.at[d, c],
            {"dp": z + 1 if direction == 0 else z - 1},
        )

    def scatter_step(n):
        for direction in (0, 1):
            behind = z if direction == 0 else nd - 1 - z
            index = n - CHUNKS - LAG * behind

            @pl.when((index >= 0) & (index < (nd - 1 - behind) * CHUNKS))
            def _():
                s, c = lax.div(index, CHUNKS), lax.rem(index, CHUNKS)
                d = nd - 1 - s if direction == 0 else s
                landing = from_left if direction == 0 else from_right
                value = partial(d, c)

                @pl.when(behind > 0)
                def _():
                    part_copy(direction, d, c).wait_recv()
                    part[d, c] = (value + landing[d, c].astype(F32)).astype(BF16)

                @pl.when(behind == 0)
                def _():
                    part[d, c] = value.astype(BF16)

                part_copy(direction, d, c).start()

    def late(n, _):
        gather_step(n, True)
        scatter_step(n)
        return 0

    def last(n, _):
        scatter_step(n)
        return 0

    grad_spread = spread("tensor", 0, lambda peer: all_grad.at[k], all_grad.at[k])
    lax.fori_loop(0, 2, early, 0)
    swap_wait(0, grad_ref, all_grad.at[z])
    start(grad_spread)
    lax.fori_loop(2, CHUNKS, early, 0)
    swap_wait(1, up_factor_ref, own_up)
    finish(grad_spread)

    tenant = owner_ref[0]
    rank = rank_ref[tenant]
    row_scale = slots / (4.0 * rank.astype(F32))
    keep = (lax.broadcasted_iota(jnp.int32, (1, slots), 1) < rank).astype(F32)

    for b in range(nd):
        back_src[b] = dot_t(all_grad[b], own_up[...]).astype(BF16)
    copies = spread("dp", 0, lambda peer: back_src.at[peer], back_dst.at[z])
    start(copies)
    back_dst[z] = back_src[z]
    finish(copies)
    total = back_dst[0].astype(F32)
    for b in range(1, nd):
        total += back_dst[b].astype(F32)
    back_own[k] = total.astype(BF16)
    copies = spread("tensor", 1, lambda peer: back_own.at[k], back_own.at[k])
    start(copies)
    finish(copies)
    mine = jnp.zeros((rows, slots), F32)
    for e in range(nt):
        mine += jnp.where(tenant == e, 1.0, 0.0) * back_own[e].astype(F32)
    mine = mine * (row_scale * keep)
    for b in range(nd):
        back_mask_src[b] = (mine * jnp.where(tenant == b, 1.0, 0.0)).astype(BF16)
    copies = spread("dp", 1, lambda peer: back_mask_src.at[peer], back_mask.at[z])
    start(copies)
    back_mask[z] = back_mask_src[z]
    finish(copies)

    lax.fori_loop(CHUNKS, (nd - 1) * CHUNKS, late, 0)

    begin = (nd - 1) * CHUNKS
    for b in range(nd):
        low_src[b] = low[b].astype(BF16)
    copies = spread("dp", 2, lambda peer: low_src.at[peer], low_dst.at[z])
    start(copies)
    low_dst[z] = low_src[z]
    lax.fori_loop(begin, begin + 1, last, 0)
    finish(copies)
    mine = jnp.zeros((rows, slots), F32)
    for e in range(nd):
        mine += jnp.where(tenant == e, 1.0, 0.0) * low_dst[e].astype(F32)
    low_own[k] = mine.astype(BF16)
    copies = spread("tensor", 2, lambda peer: low_own.at[k], low_own.at[k])
    start(copies)
    lax.fori_loop(begin + 1, begin + 2, last, 0)
    finish(copies)
    total = low_own[0].astype(F32)
    for e in range(1, nt):
        total += low_own[e].astype(F32)
    low_mask[z] = (total * keep * jnp.where(tenant == k, 1.0, 0.0)).astype(BF16)
    copies = spread("dp", 3, lambda peer: low_mask.at[z], low_mask.at[z])
    start(copies)
    lax.fori_loop(begin + 2, begin + 3, last, 0)
    finish(copies)

    k_scale = slots / (4.0 * rank_ref[k].astype(F32))
    for b in range(nt):
        base_src[b] = (base[b] + dot(low_mask[b], own_up[...]) * k_scale).astype(BF16)
    copies = spread("tensor", 3, lambda peer: base_src.at[peer], base_dst.at[k])
    start(copies)
    base_dst[k] = base_src[k]
    term = dot_0(low_mask[0], all_grad[0])
    for b in range(1, nt):
        term += dot_0(low_mask[b], all_grad[b])
    up_term[...] = (term * k_scale).astype(BF16)
    swap_start(2, up_term, up_land)
    lax.fori_loop(begin + 3, begin + 5, last, 0)
    finish(copies)
    total = base_dst[0].astype(F32)
    for b in range(1, nt):
        total += base_dst[b].astype(F32)
    out_src[...] = total.astype(BF16)
    swap_start(3, out_src, out_ref)
    lax.fori_loop(begin + 5, nd * CHUNKS, last, 0)

    def down_step(c, _):
        term = dot_0(back_mask[0], hid[0, c])
        for b in range(1, nd):
            term += dot_0(back_mask[b], hid[b, c])
        down_grad_ref[pl.ds(pl.multiple_of(c * fc, fc), fc), :] = term.T
        return 0

    lax.fori_loop(0, CHUNKS, down_step, 0)

    def finish_step(c, _):
        cols = pl.ds(pl.multiple_of(c * fc, fc), fc)
        part[z, c] = partial(z, c).astype(BF16)

        @pl.when(z > 0)
        def _():
            part_copy(0, z, c).wait_recv()
            part[z, c] = (part[z, c].astype(F32) + from_left[z, c].astype(F32)).astype(BF16)

        @pl.when(z + 1 < nd)
        def _():
            part_copy(1, z, c).wait_recv()
            part[z, c] = (part[z, c].astype(F32) + from_right[z, c].astype(F32)).astype(BF16)

        total = part[z, c].astype(F32) * live
        gate = gate_ref[:, cols].astype(F32)
        up = up_ref[:, cols].astype(F32)
        s = jax.nn.sigmoid(gate)
        gate_grad_ref[:, cols] = (total * up * s * (1.0 + gate * (1.0 - s))).astype(BF16)
        up_grad_ref[:, cols] = (total * (gate * s)).astype(BF16)
        return 0

    lax.fori_loop(0, CHUNKS, finish_step, 0)

    swap_wait(2, up_term, up_land)
    up_grad_factor_ref[...] = up_land[...].astype(F32)
    swap_wait(3, out_src, out_ref)

    def drain(n, _):
        s, c = lax.div(n, CHUNKS), lax.rem(n, CHUNKS)

        @pl.when((s <= z) & (z + 1 < nd))
        def _():
            hid_copy(0, s, c).wait_send()

        @pl.when((s >= z) & (z > 0))
        def _():
            hid_copy(1, s, c).wait_send()

        @pl.when(s > z)
        def _():
            part_copy(0, s, c).wait_send()

        @pl.when(s < z)
        def _():
            part_copy(1, s, c).wait_send()

        return 0

    lax.fori_loop(0, nd * CHUNKS, drain, 0)


def shards(
    gate_preactivation,
    up_preactivation,
    quantized_weight_levels,
    absmax,
    adapter_down_factor,
    adapter_up_factor,
    tenant_adapter_rank,
    block_owner_tenant,
    block_live_rows,
    output_gradient,
):
    nd, nt = lax.axis_size("dp"), lax.axis_size("tensor")
    rows, hidden_cols = gate_preactivation.shape
    width = output_gradient.shape[1]
    slots = adapter_down_factor.shape[2]
    fc = hidden_cols // CHUNKS
    assert nd == nt and block_owner_tenant.shape[0] == 1
    vmem = pl.BlockSpec(memory_space=pltpu.VMEM)
    smem = pl.BlockSpec(memory_space=pltpu.SMEM)

    def buffer(*shape, dtype=BF16):
        return pltpu.VMEM(shape, dtype)

    dma = pltpu.SemaphoreType.DMA
    out, gate_grad, up_grad, down_grad, up_factor_grad = pl.pallas_call(
        functools.partial(kernel, nd, nt),
        out_shape=(
            jax.ShapeDtypeStruct((rows, width), BF16),
            jax.ShapeDtypeStruct((rows, hidden_cols), BF16),
            jax.ShapeDtypeStruct((rows, hidden_cols), BF16),
            jax.ShapeDtypeStruct((hidden_cols, slots), F32),
            jax.ShapeDtypeStruct((slots, width), F32),
        ),
        in_specs=[smem] * 3 + [vmem] * 2 + [pl.BlockSpec(memory_space=pl.ANY)] + [vmem] * 4,
        out_specs=[vmem] * 5,
        scratch_shapes=[
            buffer(2, fc, width, dtype=jnp.int32),
            buffer(CHUNKS, fc, width),
            buffer(nd, CHUNKS, rows, fc),
            buffer(nt, rows, width),
            buffer(slots, width),
            buffer(nd, CHUNKS, rows, fc),
            buffer(nd, CHUNKS, rows, fc),
            buffer(nd, CHUNKS, rows, fc),
            buffer(nd, rows, width, dtype=F32),
            buffer(nd, rows, slots, dtype=F32),
            buffer(nd, rows, slots),
            buffer(nd, rows, slots),
            buffer(nt, rows, slots),
            buffer(nd, rows, slots),
            buffer(nd, rows, slots),
            buffer(nd, rows, slots),
            buffer(nd, rows, slots),
            buffer(nt, rows, slots),
            buffer(nd, rows, slots),
            buffer(nt, rows, width),
            buffer(nt, rows, width),
            buffer(rows, width),
            buffer(slots, width),
            buffer(slots, width),
            dma((2,)),
            dma((4,)),
            dma((4,)),
            dma((4,)),
            dma((2, nd, CHUNKS)),
            dma((nd, CHUNKS)),
            dma((nd, CHUNKS)),
            dma((nd, CHUNKS)),
            dma((nd, CHUNKS)),
            dma((4, nd)),
            dma((4, nd)),
            dma((4, nt)),
            dma((4, nt)),
        ],
        compiler_params=pltpu.CompilerParams(
            collective_id=0, has_side_effects=True, vmem_limit_bytes=60 << 20
        ),
        cost_estimate=pl.CostEstimate(
            flops=4 * nd * rows * hidden_cols * width,
            bytes_accessed=4 * hidden_cols * width,
            transcendentals=0,
        ),
    )(
        tenant_adapter_rank,
        block_owner_tenant,
        block_live_rows,
        gate_preactivation,
        up_preactivation,
        quantized_weight_levels,
        absmax,
        adapter_down_factor[0],
        adapter_up_factor[0],
        output_gradient,
    )
    return out, gate_grad, up_grad, down_grad[None], up_factor_grad[None]


def solution(mesh):
    placed = (
        P(("groups", "dp"), "tensor"),
        P(("groups", "dp"), "tensor"),
        P("tensor", "dp"),
        P("tensor", "dp"),
        P("dp", "tensor", None),
        P("dp", None, "tensor"),
        P(),
        P(("groups", "dp")),
        P(("groups", "dp")),
        P(("groups", "dp"), "tensor"),
    )
    return jax.shard_map(
        shards,
        mesh=mesh,
        in_specs=placed,
        out_specs=(
            P(("groups", "dp"), "tensor"),
            P(("groups", "dp"), "tensor"),
            P(("groups", "dp"), "tensor"),
            P(("groups", "dp"), "tensor", None),
            P(("groups", "dp"), None, "tensor"),
        ),
        check_vma=False,
    )
```

time: 335 us -> 173 us (0.52)
  waiting for transfers between devices: 201 us -> 0 us
  Pallas kernels: 0 us -> 156 us
  matrix products: 29.9 us -> 0 us
  other arithmetic: 29.8 us -> 0 us
  blocking collectives: 29.8 us -> 0 us
  between operations: 18 us -> 1.95 us
  local copies, waits for them, and re-layouts: 22.5 us -> 11.3 us
    pallas_call x0 -> x1, Pallas kernels: none -> 156 us  [shards(): pl.pallas_call(functools.partial(kernel, nd, nt), out_shape=(jax.ShapeDty...]
    reduce_scatter x2 -> x0, waiting for transfers between devices: 85.6 us -> none  [the longest x1 70.4 us: shards(): lax.psum_scatter(partial_grad.astype(bf16), 'dp', scatter_dimension=0, ti...]
    psum x1 -> x0, waiting for transfers between devices: 76.6 us -> none  [shards(): low_rank = lax.psum(low.astype(bf16), ('dp', 'tensor'))]
    all_gather x2 -> x0, waiting for transfers between devices: 38.7 us -> none  [the longest x1 38.7 us: shards(): all_hidden = lax.all_gather(hidden, 'dp', axis=0, tiled=True)]
    dot_general x8 -> x0, matrix products: 29.9 us -> none  [the longest x1 9.16 us: shards(): partial_out = jnp.dot(all_hidden, weight, preferred_element_type=f32)]
    unnamed x1 -> x0, blocking collectives: 29.8 us -> none
    convert_element_type x5 -> x0, other arithmetic: 25.5 us -> none  [the longest x1 19 us: dequantize(): return scaled.reshape(rows_count, cols_count).astype(jnp.bfloat16)]
    unnamed x23 -> x15, local copies, waits for them, and re-layouts: 17.9 us -> 11.3 us
  transfers between devices with their start and end apart: 8 -> 0, of which waited for: 4 -> 0; matrix products, arithmetic and copies ran while one was open for 22% -> 0% of each run, Pallas kernels for 0% -> 0%
where the time goes in v2:
time: 173 us; the launch traced here: 169 us
  Pallas kernels  156 us (90%)
  local copies, waits for them, and re-layouts  11.3 us (7%)
  between operations  1.95 us (1%)
    pallas_call x1, Pallas kernels, shards(): pl.pallas_call(functools.partial(kernel, nd, nt), out_shape=(jax.ShapeDty...  156 us
    unnamed x15, local copies, waits for them, and re-layouts  11.3 us

profile of v2, /device:TPU:0, one launch (start us, length us, event | category | flops | bytes accessed | tf_op | source)
XLA Modules:
  0.0 169.4 jit_solution(4450297266438085974)
XLA Ops:
  1.9 2.3 %copy.15 = bf16[1,3584,64]{2,1,0:T(8,128)(2,1)} copy(bf16[1,3584,64]{1,2,0:T(8,128)(2,1)} %param.14) | data formatting | bytes 917504 | tf_op args[4]
  4.2 2.7 %copy.16.absmax_ref = f32[3584,16]{1,0:T(8,128)} copy(f32[3584,16]{0,1:T(8,128)} %param.13) | data formatting | bytes 458752 | tf_op args[3]
  6.9 156.1 %shard_map.137 = (bf16[128,1024]{1,0:T(8,128)(2,1)}, bf16[128,3584]{1,0:T(8,128)(2,1)}, bf16[128,3584]{1,0:T(8,128)(2,1)}, f32[3584,64]{1,0:T(8,128)}, f32[64,1024]{1,0:T(8,128)}) custom-call(s32[4]{0:T(128)} %rank_ref.1, s32[1]{0:T(128)S(6)} %copy.22.owner_ref, s32[1]{0:T(128)S(6)} %copy.23.live_ref, bf16[128,3584]{1,0:T(8,128)(2,1)} %gate_ref.1, ...), custom_call_target="tpu_custom_call" | custom-call | flops 7516192768 | bytes 14680064 | tf_op jit(solution)/shard_map/pallas_call | solution.py:527
  163.0 0.0 copy-start.3
  163.0 0.0 copy-start.1
  163.1 3.0 %copy.17 = f32[1,3584,64]{1,2,0:T(8,128)} copy(f32[1,3584,64]{2,1,0:T(8,128)} %bitcast.4) | data formatting | bytes 1835008
  166.1 0.0 copy-done.3
  166.1 0.0 copy-start
  166.1 0.7 copy.24
  166.8 0.0 copy-done.1
  166.8 0.0 copy-start.2
  166.8 0.9 copy.25
  167.7 0.0 copy-done
  167.7 0.9 copy.26
  168.7 0.0 copy-done.2
  168.7 0.7 copy.27
Async XLA Ops:
  163.0 3.1 %copy-start.3 = (bf16[128,1024]{1,0:T(8,128)(2,1)S(1)}, bf16[128,1024]{1,0:T(8,128)(2,1)}, u32[]{:S(2)}) copy-start(bf16[128,1024]{1,0:T(8,128)(2,1)} %get-tuple-element.25) | copy-start | bytes 786436
  163.0 3.8 %copy-start.1 = (bf16[128,3584]{1,0:T(8,128)(2,1)S(1)}, bf16[128,3584]{1,0:T(8,128)(2,1)}, u32[]{:S(2)}) copy-start(bf16[128,3584]{1,0:T(8,128)(2,1)} %get-tuple-element.26) | copy-start | bytes 2752516
  166.1 1.6 copy-start
  166.8 1.9 %copy-start.2 = (f32[64,1024]{1,0:T(8,128)S(1)}, f32[64,1024]{1,0:T(8,128)}, u32[]{:S(2)}) copy-start(f32[64,1024]{1,0:T(8,128)} %get-tuple-element.14) | copy-start | bytes 786436

commit v3 on v2

--- a/solution.py
+++ b/solution.py
@@ -11,6 +11,7 @@
 F32, BF16 = jnp.float32, jnp.bfloat16
 CHUNKS = 7
 LAG = 2
+FLIGHT = 2
 
 nf4_levels = (
     -1.0,
@@ -71,6 +72,7 @@
     down_grad_ref,
     up_grad_factor_ref,
     codes,
+    scales,
     weight,
     hid,
     all_grad,
@@ -111,7 +113,7 @@
     z, k = lax.axis_index("dp"), lax.axis_index("tensor")
     rows, hidden_cols = gate_ref.shape
     width = grad_ref.shape[1]
-    slots = down_ref.shape[1]
+    slots = down_ref.shape[0]
     fc = hidden_cols // CHUNKS
     off_diagonal = z != k
 
@@ -229,19 +231,18 @@
 
         return 0
 
-    lax.fori_loop(0, CHUNKS, make_hidden, 0)
-
     tile = 32
-    blocks_per_scale = width // absmax_ref.shape[1]
+    blocks_per_scale = width // absmax_ref.shape[0]
     lanes = lax.broadcasted_iota(jnp.int32, (tile, 128), 1)
 
     def dequantize(c):
+        scales[...] = absmax_ref[:, pl.ds(pl.multiple_of(c * fc, fc), fc)].T
         code_copy(c).wait()
         slot = lax.rem(c, 2)
 
         def step(t, _):
             r = pl.ds(pl.multiple_of(t * tile, tile), tile)
-            scale = absmax_ref[pl.ds(pl.multiple_of(c * fc + t * tile, tile), tile), :]
+            scale = scales[r, :]
             for g in range(width // 128):
                 cols = slice(g * 128, (g + 1) * 128)
                 per = 128 // blocks_per_scale
@@ -263,7 +264,7 @@
 
     def forward(s, c, first):
         value = hid[s, c]
-        down = down_ref[pl.ds(pl.multiple_of(c * fc, fc), fc), :]
+        down = down_ref[:, pl.ds(pl.multiple_of(c * fc, fc), fc)]
         if first:
 
             @pl.when(c == 0)
@@ -272,7 +273,7 @@
                 low[s] = jnp.zeros((rows, slots), F32)
 
         base[s] += dot(value, weight[c])
-        low[s] += dot(value, down)
+        low[s] += dot_t(value, down)
 
     def gather_step(n, first):
         h = 1 + lax.div(n, CHUNKS)
@@ -303,14 +304,15 @@
             forward(z + h, c, True)
 
     def early(n, _):
+        make_hidden(n, 0)
         dequantize(n)
         forward(z, n, True)
         gather_step(n, True)
         return 0
 
     def partial(d, c):
-        down = down_ref[pl.ds(pl.multiple_of(c * fc, fc), fc), :]
-        return dot_t(all_grad[d], weight[c]) + dot_t(back_mask[d], down)
+        down = down_ref[:, pl.ds(pl.multiple_of(c * fc, fc), fc)]
+        return dot_t(all_grad[d], weight[c]) + dot(back_mask[d], down)
 
     def part_copy(direction, d, c):
         landing, recv = (from_left, left_recv) if direction == 0 else (from_right, right_recv)
@@ -334,6 +336,13 @@
                 landing = from_left if direction == 0 else from_right
                 value = partial(d, c)
 
+                @pl.when(index >= FLIGHT)
+                def _():
+                    old = index - FLIGHT
+                    old_s = lax.div(old, CHUNKS)
+                    old_d = nd - 1 - old_s if direction == 0 else old_s
+                    part_copy(direction, old_d, lax.rem(old, CHUNKS)).wait_send()
+
                 @pl.when(behind > 0)
                 def _():
                     part_copy(direction, d, c).wait_recv()
@@ -358,7 +367,7 @@
     lax.fori_loop(0, 2, early, 0)
     swap_wait(0, grad_ref, all_grad.at[z])
     start(grad_spread)
-    lax.fori_loop(2, CHUNKS, early, 0)
+    lax.fori_loop(2, 4, early, 0)
     swap_wait(1, up_factor_ref, own_up)
     finish(grad_spread)
 
@@ -372,6 +381,7 @@
     copies = spread("dp", 0, lambda peer: back_src.at[peer], back_dst.at[z])
     start(copies)
     back_dst[z] = back_src[z]
+    lax.fori_loop(4, 5, early, 0)
     finish(copies)
     total = back_dst[0].astype(F32)
     for b in range(1, nd):
@@ -379,6 +389,7 @@
     back_own[k] = total.astype(BF16)
     copies = spread("tensor", 1, lambda peer: back_own.at[k], back_own.at[k])
     start(copies)
+    lax.fori_loop(5, 6, early, 0)
     finish(copies)
     mine = jnp.zeros((rows, slots), F32)
     for e in range(nt):
@@ -389,6 +400,7 @@
     copies = spread("dp", 1, lambda peer: back_mask_src.at[peer], back_mask.at[z])
     start(copies)
     back_mask[z] = back_mask_src[z]
+    lax.fori_loop(6, CHUNKS, early, 0)
     finish(copies)
 
     lax.fori_loop(CHUNKS, (nd - 1) * CHUNKS, late, 0)
@@ -442,7 +454,7 @@
         term = dot_0(back_mask[0], hid[0, c])
         for b in range(1, nd):
             term += dot_0(back_mask[b], hid[b, c])
-        down_grad_ref[pl.ds(pl.multiple_of(c * fc, fc), fc), :] = term.T
+        down_grad_ref[:, pl.ds(pl.multiple_of(c * fc, fc), fc)] = term
         return 0
 
     lax.fori_loop(0, CHUNKS, down_step, 0)
@@ -486,11 +498,11 @@
         def _():
             hid_copy(1, s, c).wait_send()
 
-        @pl.when(s > z)
+        @pl.when((s == z + 1) & (c >= CHUNKS - FLIGHT))
         def _():
             part_copy(0, s, c).wait_send()
 
-        @pl.when(s < z)
+        @pl.when((s == z - 1) & (c >= CHUNKS - FLIGHT))
         def _():
             part_copy(1, s, c).wait_send()
 
@@ -530,13 +542,14 @@
             jax.ShapeDtypeStruct((rows, width), BF16),
             jax.ShapeDtypeStruct((rows, hidden_cols), BF16),
             jax.ShapeDtypeStruct((rows, hidden_cols), BF16),
-            jax.ShapeDtypeStruct((hidden_cols, slots), F32),
+            jax.ShapeDtypeStruct((slots, hidden_cols), F32),
             jax.ShapeDtypeStruct((slots, width), F32),
         ),
         in_specs=[smem] * 3 + [vmem] * 2 + [pl.BlockSpec(memory_space=pl.ANY)] + [vmem] * 4,
         out_specs=[vmem] * 5,
         scratch_shapes=[
             buffer(2, fc, width, dtype=jnp.int32),
+            buffer(fc, absmax.shape[1], dtype=F32),
             buffer(CHUNKS, fc, width),
             buffer(nd, CHUNKS, rows, fc),
             buffer(nt, rows, width),
@@ -589,12 +602,12 @@
         gate_preactivation,
         up_preactivation,
         quantized_weight_levels,
-        absmax,
-        adapter_down_factor[0],
+        absmax.T,
+        adapter_down_factor[0].T,
         adapter_up_factor[0],
         output_gradient,
     )
-    return out, gate_grad, up_grad, down_grad[None], up_factor_grad[None]
+    return out, gate_grad, up_grad, down_grad.T[None], up_factor_grad[None]
 
 
 def solution(mesh):

time: 173 us -> 171 us (0.988)
  the two profiles are of different devices: /device:TPU:0 before, /device:TPU:21 now
where the time goes in v3:
time: 171 us
  Pallas kernels  159 us (93%)
  local copies, waits for them, and re-layouts  9.83 us (6%)
  between operations  1.94 us (1%)
    pallas_call x1, Pallas kernels, shards(): pl.pallas_call(functools.partial(kernel, nd, nt), out_shape=(jax.ShapeDty...  159 us
    unnamed x5, local copies, waits for them, and re-layouts  9.83 us

profile of v3, /device:TPU:21, one launch (start us, length us, event | category | flops | bytes accessed | tf_op | source)
XLA Modules:
  0.0 171.0 jit_solution(16766668279980426491)
XLA Ops:
  1.9 159.3 %shard_map.137 = (bf16[128,1024]{1,0:T(8,128)(2,1)}, bf16[128,3584]{1,0:T(8,128)(2,1)}, bf16[128,3584]{1,0:T(8,128)(2,1)}, f32[64,3584]{1,0:T(8,128)}, f32[64,1024]{1,0:T(8,128)}) custom-call(s32[4]{0:T(128)} %rank_ref.1, s32[1]{0:T(128)S(6)} %copy.20.owner_ref, s32[1]{0:T(128)S(6)} %copy.21.live_ref, bf16[128,3584]{1,0:T(8,128)(2,1)} %gate_ref.1, ...), custom_call_target="tpu_custom_call" | custom-call | flops 7516192768 | bytes 14680064 | tf_op jit(solution)/shard_map/pallas_call | solution.py:539
  161.2 1.7 copy.22
  162.9 2.2 %copy.23 = bf16[128,3584]{1,0:T(8,128)(2,1)} copy(bf16[128,3584]{1,0:T(8,128)(2,1)} %get-tuple-element.21) | data formatting | bytes 1835008
  165.1 2.2 %copy.24 = bf16[128,3584]{1,0:T(8,128)(2,1)} copy(bf16[128,3584]{1,0:T(8,128)(2,1)} %get-tuple-element.22) | data formatting | bytes 1835008
  167.2 2.2 %copy.25 = f32[1,3584,64]{1,2,0:T(8,128)} copy(f32[1,3584,64]{1,2,0:T(8,128)} %bitcast.9) | data formatting | bytes 1835008
  169.4 1.7 copy.26

commit v4 on v3

--- a/solution.py
+++ b/solution.py
@@ -10,8 +10,9 @@
 MESH = pl.DeviceIdType.MESH
 F32, BF16 = jnp.float32, jnp.bfloat16
 CHUNKS = 7
-LAG = 2
-FLIGHT = 2
+LAG = 4
+FLIGHT = 4
+AHEAD = 3
 
 nf4_levels = (
     -1.0,
@@ -275,7 +276,7 @@
         base[s] += dot(value, weight[c])
         low[s] += dot_t(value, down)
 
-    def gather_step(n, first):
+    def gather_send(n):
         h = 1 + lax.div(n, CHUNKS)
         c = lax.rem(n, CHUNKS)
 
@@ -295,6 +296,10 @@
             def _():
                 hid_copy(1, z + h, c).start()
 
+    def gather_use(n):
+        h = 1 + lax.div(n, CHUNKS)
+        c = lax.rem(n, CHUNKS)
+
         @pl.when(z - h >= 0)
         def _():
             forward(z - h, c, True)
@@ -304,10 +309,14 @@
             forward(z + h, c, True)
 
     def early(n, _):
-        make_hidden(n, 0)
+        @pl.when(n + AHEAD < CHUNKS)
+        def _():
+            make_hidden(n + AHEAD, 0)
+
         dequantize(n)
+        gather_send(n)
         forward(z, n, True)
-        gather_step(n, True)
+        gather_use(n)
         return 0
 
     def partial(d, c):
@@ -355,14 +364,16 @@
                 part_copy(direction, d, c).start()
 
     def late(n, _):
-        gather_step(n, True)
+        gather_send(n)
         scatter_step(n)
+        gather_use(n)
         return 0
 
     def last(n, _):
         scatter_step(n)
         return 0
 
+    lax.fori_loop(0, AHEAD, make_hidden, 0)
     grad_spread = spread("tensor", 0, lambda peer: all_grad.at[k], all_grad.at[k])
     lax.fori_loop(0, 2, early, 0)
     swap_wait(0, grad_ref, all_grad.at[z])

time: 171 us -> 166 us (0.971)
  the two profiles are of different devices: /device:TPU:21 before, /device:TPU:0 now
where the time goes in v4:
time: 166 us; the launch traced here: 165 us
  Pallas kernels  154 us (93%)
  local copies, waits for them, and re-layouts  9.83 us (6%)
  between operations  1.94 us (1%)
    pallas_call x1, Pallas kernels, shards(): pl.pallas_call(functools.partial(kernel, nd, nt), out_shape=(jax.ShapeDty...  154 us
    unnamed x5, local copies, waits for them, and re-layouts  9.83 us

profile of v4, /device:TPU:0, one launch (start us, length us, event | category | flops | bytes accessed | tf_op | source)
XLA Modules:
  0.0 165.4 jit_solution(13979473953569231798)
XLA Ops:
  1.9 153.6 %shard_map.137 = (bf16[128,1024]{1,0:T(8,128)(2,1)}, bf16[128,3584]{1,0:T(8,128)(2,1)}, bf16[128,3584]{1,0:T(8,128)(2,1)}, f32[64,3584]{1,0:T(8,128)}, f32[64,1024]{1,0:T(8,128)}) custom-call(s32[4]{0:T(128)} %rank_ref.1, s32[1]{0:T(128)S(6)} %copy.20.owner_ref, s32[1]{0:T(128)S(6)} %copy.21.live_ref, bf16[128,3584]{1,0:T(8,128)(2,1)} %gate_ref.1, ...), custom_call_target="tpu_custom_call" | custom-call | flops 7516192768 | bytes 14680064 | tf_op jit(solution)/shard_map/pallas_call | solution.py:550
  155.5 1.7 %copy.22 = bf16[128,1024]{1,0:T(8,128)(2,1)} copy(bf16[128,1024]{1,0:T(8,128)(2,1)} %get-tuple-element.20) | data formatting | bytes 524288
  157.2 2.2 %copy.23 = bf16[128,3584]{1,0:T(8,128)(2,1)} copy(bf16[128,3584]{1,0:T(8,128)(2,1)} %get-tuple-element.21) | data formatting | bytes 1835008
  159.4 2.2 %copy.24 = bf16[128,3584]{1,0:T(8,128)(2,1)} copy(bf16[128,3584]{1,0:T(8,128)(2,1)} %get-tuple-element.22) | data formatting | bytes 1835008
  161.5 2.2 %copy.25 = f32[1,3584,64]{1,2,0:T(8,128)} copy(f32[1,3584,64]{1,2,0:T(8,128)} %bitcast.9) | data formatting | bytes 1835008
  163.7 1.7 %copy.26 = f32[1,64,1024]{2,1,0:T(8,128)} copy(f32[1,64,1024]{2,1,0:T(8,128)} %bitcast.10) | data formatting | bytes 524288
